TPU v7x, 32 devices: a whole 2x2x4 slice. The times are simulated.
32 devices in a mesh: seq: 16 (over z, y, core), ch: 2 (over x).
Axes of the slice: x: 2, y: 2, z: 4, core: 2. Of those that a mesh axis runs over, the one named last changes fastest.
Arguments:
- tokens: int32 [4096], P('seq'), may hold values from 0 to 3
- feature_table: bfloat16 [512, 3, 4096], P(None, None, 'ch'), may hold values from -6 to 6
- short_filter: float32 [3, 7, 4096], P(None, None, 'ch'), may hold values from -2 to 2
- med_filter: bfloat16 [128, 256], P(None, 'ch'), may hold values from -0.5 to 0.5
- med_bias: float32 [4096], P('ch'), may hold values from 0.5 to 1.5
- out_weight: bfloat16 [4096, 4096], P('seq', 'ch'), may hold values from -0.09375 to 0.09375
Outputs:
- scored: bfloat16 [4096, 4096], P('seq', 'ch')
All inputs are finite; a program needn't handle non-finite values.
Results may differ from a plain program's by a relative error of at most 0.01.
Values may be sent and summed in bfloat16 or wider, within the bound.
A program may use at most 128 MiB of HBM per device.

v0:
```python
import jax
import jax.numpy as jnp
import numpy as np
from jax import lax
from jax.sharding import PartitionSpec as P

base_codes = np.array([65, 67, 71, 84], dtype=np.int32)


def from_behind(value, axis, steps):
    count = lax.axis_size(axis)
    initial, last = (max(0, -steps), min(count, count - steps))
    return lax.ppermute(value, axis, [(source, source + steps) for source in range(initial, last)])


def rims(forward_rows, reverse_rows, rim_width):
    start_row = forward_rows.shape[0] - rim_width
    forward = from_behind(forward_rows[start_row:], "seq", 1)
    second = from_behind(reverse_rows[start_row:], "seq", -1)
    return jnp.stack([forward, second])


def toeplitz(filters):
    tap_count = filters.shape[0]
    row_index = jnp.arange(tap_count, dtype=jnp.int32)[:, None]
    col_index = jnp.arange(2 * tap_count - 1, dtype=jnp.int32)[None, :]
    tap_index = row_index - col_index + tap_count - 1
    inside = (tap_index >= 0) & (tap_index < tap_count)
    picked = jnp.take(filters, jnp.clip(tap_index, 0, tap_count - 1), axis=0)
    toeplitz_table = jnp.where(inside[:, :, None], picked, jnp.zeros((), filters.dtype))
    return jnp.transpose(toeplitz_table, (2, 0, 1))


def per_device(tokens, feature_table, short_filter, med_filter, med_bias, out_weight):
    length = tokens.shape[0]
    width_local = feature_table.shape[2]
    short_taps = short_filter.shape[1]
    tap_count = med_filter.shape[0]
    groups_local = med_filter.shape[1]
    group_width = width_local // groups_local
    strand_bases = jnp.stack([tokens, 3 - jnp.flip(tokens, 0)])
    corner = feature_table[base_codes]
    features = jnp.take(corner, strand_bases, axis=0)
    short_rim = rims(features[0], features[1], short_taps - 1)
    extended = jnp.concatenate([short_rim, features], axis=1).astype(jnp.float32)
    short_out = jnp.zeros((2, length, 3, width_local), jnp.float32)
    for shift_index in range(short_taps):
        begin = short_taps - 1 - shift_index
        short_out = (
            short_out + short_filter[:, shift_index, :] * extended[:, begin : begin + length]
        )
    gated_mix = (short_out[:, :, 0] * short_out[:, :, 2]).astype(jnp.bfloat16)
    medium_rim = rims(gated_mix[0], gated_mix[1], tap_count - 1)
    padded = jnp.concatenate([medium_rim, gated_mix], axis=1)
    kernel = toeplitz(med_filter)
    block_count = length // tap_count
    windows = jnp.stack(
        [
            padded[:, block_index * tap_count : block_index * tap_count + 2 * tap_count - 1]
            for block_index in range(block_count)
        ],
        axis=1,
    )
    windows = windows.reshape(2, block_count, 2 * tap_count - 1, groups_local, group_width)
    medium = jnp.einsum("grw,snwgc->snrgc", kernel, windows, preferred_element_type=jnp.float32)
    medium = medium.reshape(2, length, width_local) + med_bias * gated_mix.astype(jnp.float32)
    hidden = (short_out[:, :, 1] * medium).astype(jnp.bfloat16)
    reverse = hidden[1]
    averaged = (
        0.5 * (hidden[0].astype(jnp.float32) + jnp.flip(reverse, 0).astype(jnp.float32))
    ).astype(jnp.bfloat16)
    gathered = lax.all_gather(averaged, "ch", axis=1, tiled=True)
    weight_rows = lax.all_gather(out_weight, "seq", axis=0, tiled=True)
    result = jnp.dot(gathered, weight_rows, preferred_element_type=jnp.float32)
    return result.astype(jnp.bfloat16)


def solution(mesh):
    placed = (
        P("seq"),
        P(None, None, "ch"),
        P(None, None, "ch"),
        P(None, "ch"),
        P("ch"),
        P("seq", "ch"),
    )
    return jax.shard_map(
        per_device, mesh=mesh, in_specs=placed, out_specs=P("seq", "ch"), check_vma=False
    )
```

profile of v0, /device:TPU:0, one launch (start us, length us, event | category | flops | bytes accessed | tf_op | source)
XLA Modules:
  0.0 461.9 jit_solution(11697910313658378829)
XLA Ops:
  6.5 0.0 all-gather.3.cloned.1.call-start
  6.5 0.7 pad_clamp_fusion.2
  7.2 1.6 gather_fusion
  8.8 0.8 rev.8
  9.6 0.7 compare_select_fusion.2
  10.3 17.1 %gather_fusion.1 = bf16[512,3,2048]{2,1,0:T(4,128)(2,1)} fusion(bf16[4,3,2048]{2,1,0:T(4,128)(2,1)S(1)} %copy.31, s32[1024]{0:T(1024)S(1)} %pad_clamp_fusion.1), kind=kCustom, calls=%fused_computation.1 | custom fusion | bytes 12584960 | tf_op jit(solution)/shard_map/jit(_take)/gather | solution.py:43
  27.4 13.0 %copy.32 = bf16[2,256,3,2048]{1,3,0,2:T(8,128)(2,1)} copy(bf16[2,256,3,2048]{3,2,1,0:T(4,128)(2,1)} %bitcast.65) | data formatting | bytes 12582912 | tf_op jit(solution)/shard_map/jit(_take)/gather | solution.py:43
  40.4 3.3 broadcast_select_fusion
  43.7 2.6 copy-done.2
  46.4 0.9 slice_bitcast_fusion.2
  47.3 0.7 copy.35
  48.0 1.3 collective-permute-start.1
  49.3 0.7 copy.33
  50.0 3.7 collective-permute-start
  53.8 0.1 fusion.23
  53.9 0.3 reshape.198
  54.3 65.9 %gather_fusion.2 = bf16[32640,128]{1,0:T(8,128)(2,1)} fusion(bf16[128,128]{1,0:T(8,128)(2,1)S(1)} %copy-done, s32[32768]{0:T(1024)S(1)} %pad_clamp_fusion), kind=kCustom, calls=%fused_computation.2 | custom fusion | bytes 16842240 | tf_op jit(solution)/shard_map/jit(_take)/gather | solution.py:29
  120.2 9.7 %reshape.197 = bf16[128,255,128]{2,1,0:T(8,128)(2,1)} reshape(bf16[32640,128]{1,0:T(8,128)(2,1)} %gather_fusion.2) | data formatting | bytes 16711680 | tf_op jit(solution)/shard_map/jit(_take)/gather | solution.py:29
  130.1 0.1 fusion.21
  130.1 0.0 collective-permute-done.1
  130.2 0.9 copy.36
  131.1 0.0 collective-permute-done
  131.1 1.7 copy.34
  132.7 10.5 %maximum_convert_fusion = f32[2,262,3,2048]{1,3,0,2:T(8,128)} fusion(bf16[2,256,3,2048]{1,3,0,2:T(8,128)(2,1)} %copy-done.2, bf16[1,6,3,2048]{1,3,0,2:T(8,128)(2,1)S(1)} %bitcast.68, bf16[1,6,3,2048]{1,3,0,2:T(8,128)(2,1)S(1)} %bitcast.69), kind=kLoop, calls=%fused_computation.16 | loop fusion | flops 19316736 | bytes 19316736 | tf_op jit(solution)/shard_map/convert_element_type | solution.py:45
  143.2 46.7 %fusion = f32[2,256,3,2048]{1,3,0,2:T(8,128)} fusion(f32[2,262,3,2048]{1,3,0,2:T(8,128)} %maximum_convert_fusion, f32[3,2048]{1,0:T(4,128)S(1)} %get-tuple-element.18, f32[3,2048]{1,0:T(4,128)S(1)} %get-tuple-element.19, f32[3,2048]{1,0:T(4,128)S(1)} %get-tuple-element.20, f32[3,2048]{1,0:T(4,128)S(1)} %get-tuple-element.21, ...), kind=kLoop, calls=%fused_computation.4 | loop fusion | flops 40894464 | bytes 100835328 | tf_op jit(solution)/shard_map/add | solution.py:50
  189.8 3.9 fusion.14
  193.8 1.4 copy-done.4
  195.2 1.3 slice_bitcast_fusion.6
  196.5 1.3 collective-permute-start.3
  197.8 4.9 %collective-permute-start.2 = (bf16[127,2048]{0,1:T(8,128)(2,1)}, bf16[127,2048]{0,1:T(8,128)(2,1)S(1)}, u32[]{:S(2)}, u32[]{:S(2)}) collective-permute-start(bf16[127,2048]{0,1:T(8,128)(2,1)} %get-tuple-element.9), channel_id=1, source_target_pairs={{0,2},{2,4},{4,6},{6,8},{8,10},{10,12},{12,14},{14,16},{16,18},{18... | collective-permute-start | bytes 1560584 | tf_op jit(solution)/shard_map/ppermute | solution.py:13
  202.7 13.6 %select_bitcast_fusion = bf16[128,128,255,1,1]{0,2,1,4,3:T(8,128)(2,1)} fusion(bf16[128,255,128]{2,1,0:T(8,128)(2,1)} %reshape.197, pred[128,255]{1,0:T(8,128)(4,1)S(1)} %get-tuple-element.24, pred[128,255]{1,0:T(8,128)(4,1)S(1)} %get-tuple-element.25), kind=kLoop, calls=%fused_computation.17 | loop fusion | flops 8355840 | bytes 16776960 | tf_op jit(solution)/shard_map/jit(_where)/select_n | solution.py:30
  216.3 12.7 %copy.41 = bf16[128,128,255,1,1]{2,1,4,3,0:T(8,128)(2,1)} copy(bf16[128,128,255,1,1]{0,2,1,4,3:T(8,128)(2,1)} %select_bitcast_fusion) | data formatting | bytes 16711680 | tf_op jit(solution)/shard_map/jit(_where)/select_n | solution.py:30
  229.0 0.0 collective-permute-done.3
  229.0 0.0 collective-permute-done.2
  229.0 6.0 %pad_maximum_fusion.1 = (bf16[2,255,2048]{1,2,0:T(8,128)(2,1)}, bf16[2,255,2048]{1,2,0:T(8,128)(2,1)}) fusion(bf16[2,256,2048]{1,2,0:T(8,128)(2,1)} %copy-done.4, bf16[1,127,2048]{1,2,0:T(8,128)(2,1)S(1)} %bitcast.70, bf16[1,127,2048]{1,2,0:T(8,128)(2,1)S(1)} %bitcast.71), kind=kLoop, calls=%fused_computation.30 | loop fusion | flops 6266880 | bytes 9412608 | tf_op jit(solution)/shard_map/concatenate | solution.py:54
  235.0 7.2 %fusion.11 = f32[2,2,128,128,16]{2,4,1,0,3:T(8,128)} fusion(bf16[128,128,255,1,1]{2,1,4,3,0:T(8,128)(2,1)S(1)} %copy-done.3, bf16[2,1,255,128,16]{2,4,3,0,1:T(8,128)(2,1)} %bitcast.67, bf16[2,1,255,128,16]{2,4,3,0,1:T(8,128)(2,1)} %bitcast.66), kind=kOutput, calls=%fused_computation.28 | convolution fusion | flops 536862720 | bytes 16728064 | tf_op jit(solution)/shard_map/grw,snwgc->snrgc/dot_general | solution.py:65
  242.3 6.4 %copy.40 = f32[2,2,128,128,16]{2,1,4,3,0:T(2,128)} copy(f32[2,2,128,128,16]{2,4,1,0,3:T(8,128)} %fusion.11) | data formatting | bytes 8388608 | tf_op jit(solution)/shard_map/grw,snwgc->snrgc/transpose | solution.py:65
  248.7 6.4 %reshape.178 = f32[2,256,2048]{1,2,0:T(8,128)} reshape(f32[2,2,128,128,16]{2,1,4,3,0:T(2,128)} %copy.40) | data formatting | bytes 8388608 | tf_op jit(solution)/shard_map/reshape | solution.py:66
  255.1 6.3 %fusion.8 = bf16[2,256,2048]{1,2,0:T(8,128)(2,1)S(1)} fusion(f32[2,256,3,2048]{1,3,0,2:T(8,128)} %fusion, f32[2,256,2048]{1,2,0:T(8,128)} %reshape.178, f32[2048]{0:T(1024)S(1)} %copy-done.7), kind=kLoop, calls=%fused_computation.23 | loop fusion | flops 7340032 | bytes 18882560 | tf_op jit(solution)/shard_map/convert_element_type | solution.py:67
  261.4 1.0 slice_bitcast_fusion.3
  262.5 13.7 %rev.9 = bf16[256,2048]{0,1:T(8,128)(2,1)S(1)} reverse(bf16[256,2048]{0,1:T(8,128)(2,1)} %slice_bitcast_fusion.3), dimensions={0} | reverse | bytes 2097152 | tf_op jit(solution)/shard_map/jit(_flip)/rev | solution.py:70
  276.2 1.3 fusion.16
  277.5 0.0 all-gather.3.cloned.1.call-update
  277.5 0.0 all-gather.5.cloned.1.call-start
  277.5 0.7 all-gather.5.cloned.1.call-update
  278.2 35.9 %all-gather.3.cloned.1.call-done = bf16[256,4096]{0,1:T(8,128)(2,1)} async-done(((bf16[256,2048]{0,1:T(8,128)(2,1)}), bf16[256,4096]{0,1:T(8,128)(2,1)}) %all-gather.3.cloned.1.call-update) | async-done | bytes 2097168 | tf_op jit(solution)/shard_map/all_gather | solution.py:72
  314.1 129.1 %all-gather.5.cloned.1.call-done = bf16[4096,2048]{1,0:T(8,128)(2,1)} async-done(((bf16[256,2048]{1,0:T(8,128)(2,1)}), bf16[4096,2048]{1,0:T(8,128)(2,1)}) %all-gather.5.cloned.1.call-update) | async-done | bytes 16777232 | tf_op jit(solution)/shard_map/all_gather | solution.py:73
  443.2 11.9 %convolution_convert_fusion = bf16[256,2048]{1,0:T(8,128)(2,1)} fusion(bf16[256,4096]{0,1:T(8,128)(2,1)} %all-gather.3.cloned.1.call-done, bf16[4096,2048]{1,0:T(8,128)(2,1)} %all-gather.5.cloned.1.call-done), kind=kOutput, calls=%fused_computation.27 | convolution fusion | flops 4295491584 | bytes 19922944 | tf_op jit(solution)/shard_map/dot_general | solution.py:74
  (24 shorter events, 0.3 us)
Async XLA Ops:
  6.5 47.8 %copy-start = (bf16[128,128]{1,0:T(8,128)(2,1)S(1)}, bf16[128,128]{1,0:T(8,128)(2,1)}, u32[]{:S(2)}) copy-start(bf16[128,128]{1,0:T(8,128)(2,1)} %param.11) | copy-start | bytes 98308
  6.5 307.6 %all-gather.3.cloned.1.call-start = ((), (), s32[]{:S(2)}) async-start(), calls=%async_computation | async-start | bytes 3145728 | tf_op jit(solution)/shard_map/all_gather | solution.py:72
  27.3 13.0 %copy-start.6 = (s32[256]{0:T(256)S(1)}, s32[256]{0:T(256)}, u32[]{:S(2)}) copy-start(s32[256]{0:T(256)} %param.8) | copy-start | bytes 3076
  43.7 2.6 copy-start.2
  46.4 7.4 %copy-start.5 = (f32[3,7,2048]{2,1,0:T(8,128)S(1)}, f32[3,7,2048]{2,1,0:T(8,128)}, u32[]{:S(2)}) copy-start(f32[3,7,2048]{2,1,0:T(8,128)} %param.10) | copy-start | bytes 516100
  48.0 82.1 %collective-permute-start.1 = (bf16[6,3,2048]{2,0,1:T(8,128)(2,1)S(1)}, bf16[6,3,2048]{2,0,1:T(8,128)(2,1)S(1)}, u32[]{:S(2)}, u32[]{:S(2)}) collective-permute-start(bf16[6,3,2048]{2,0,1:T(8,128)(2,1)S(1)} %copy.35), channel_id=1, source_target_pairs={{2,0},{4,2},{6,4},{8,6},{10,8},{12,10},{14,12},{16,14},{18,16},{20... | collective-permute-start | bytes 221192 | tf_op jit(solution)/shard_map/ppermute | solution.py:13
  50.0 81.0 %collective-permute-start = (bf16[6,3,2048]{2,0,1:T(8,128)(2,1)S(1)}, bf16[6,3,2048]{2,0,1:T(8,128)(2,1)}, u32[]{:S(2)}, u32[]{:S(2)}) collective-permute-start(bf16[6,3,2048]{2,0,1:T(8,128)(2,1)S(1)} %copy.33), channel_id=1, source_target_pairs={{0,2},{2,4},{4,6},{6,8},{8,10},{10,12},{12,14},{14,16},{16,18},{18... | collective-permute-start | bytes 221192 | tf_op jit(solution)/shard_map/ppermute | solution.py:13
  193.8 1.4 copy-start.4
  196.5 32.5 %collective-permute-start.3 = (bf16[127,2048]{0,1:T(8,128)(2,1)}, bf16[127,2048]{0,1:T(8,128)(2,1)S(1)}, u32[]{:S(2)}, u32[]{:S(2)}) collective-permute-start(bf16[127,2048]{0,1:T(8,128)(2,1)} %get-tuple-element.10), channel_id=1, source_target_pairs={{2,0},{4,2},{6,4},{8,6},{10,8},{12,10},{14,12},{16,14},{18,16},{20... | collective-permute-start | bytes 1560584 | tf_op jit(solution)/shard_map/ppermute | solution.py:13
  197.8 31.2 %collective-permute-start.2 = (bf16[127,2048]{0,1:T(8,128)(2,1)}, bf16[127,2048]{0,1:T(8,128)(2,1)S(1)}, u32[]{:S(2)}, u32[]{:S(2)}) collective-permute-start(bf16[127,2048]{0,1:T(8,128)(2,1)} %get-tuple-element.9), channel_id=1, source_target_pairs={{0,2},{2,4},{4,6},{6,8},{8,10},{10,12},{12,14},{14,16},{16,18},{18... | collective-permute-start | bytes 1560584 | tf_op jit(solution)/shard_map/ppermute | solution.py:13
  229.0 6.0 %copy-start.3 = (bf16[128,128,255,1,1]{2,1,4,3,0:T(8,128)(2,1)S(1)}, bf16[128,128,255,1,1]{2,1,4,3,0:T(8,128)(2,1)}, u32[]{:S(2)}) copy-start(bf16[128,128,255,1,1]{2,1,4,3,0:T(8,128)(2,1)} %copy.41) | copy-start | bytes 25067524
  248.7 6.4 %copy-start.7 = (f32[2048]{0:T(1024)S(1)}, f32[2048]{0:T(1024)}, u32[]{:S(2)}) copy-start(f32[2048]{0:T(1024)} %param.12) | copy-start | bytes 24580
  277.5 165.7 %all-gather.5.cloned.1.call-start = ((), (), s32[]{:S(2)}) async-start(), calls=%async_computation.1 | async-start | bytes 17825792 | tf_op jit(solution)/shard_map/all_gather | solution.py:73
  443.2 11.9 %copy-start.1 = (bf16[128,128]{1,0:T(8,128)(2,1)S(1)}, bf16[128,128]{1,0:T(8,128)(2,1)}, u32[]{:S(2)}) copy-start(bf16[128,128]{1,0:T(8,128)(2,1)} %param.11) | copy-start | bytes 98308
Sparse Core Ops, SparseCore 0:
  277.6 36.4 all-gather.2
  316.3 126.8 all-gather.4
where the time goes:
time: 465 us; the launch traced here: 462 us
  waiting for transfers between devices  166 us (36%)
  local copies, waits for them, and re-layouts  159 us (34%)
  other arithmetic  93.2 us (20%)
  matrix products  19.1 us (4%)
  between operations  13.6 us (3%)
  starting transfers between devices  11.2 us (2%)
    all_gather x1, waiting for transfers between devices, per_device(): weight_rows = lax.all_gather(out_weight, 'seq', axis=0, tiled=True)  129 us
    gather x2, local copies, waits for them, and re-layouts, toeplitz(): picked = jnp.take(filters, jnp.clip(tap_index, 0, tap_count - 1), axis=0)  75.7 us
    add x1, other arithmetic, per_device(): short_out + short_filter[:, shift_index, :] * extended[:, begin:begin + l...  46.7 us
    all_gather x1, waiting for transfers between devices, per_device(): gathered = lax.all_gather(averaged, 'ch', axis=1, tiled=True)  35.9 us
    gather x2, local copies, waits for them, and re-layouts, per_device(): features = jnp.take(corner, strand_bases, axis=0)  30.1 us
    rev x1, local copies, waits for them, and re-layouts, per_device(): jnp.flip(reverse, 0).astype(jnp.float32)  13.7 us
    select_n x1, other arithmetic, toeplitz(): jnp.where(inside[:, :, None], picked, jnp.zeros((), filters.dtype))  13.6 us
    select_n x1, local copies, waits for them, and re-layouts, toeplitz(): jnp.where(inside[:, :, None], picked, jnp.zeros((), filters.dtype))  12.7 us
  transfers between devices with their start and end apart: 6, of which 2 were waited for; matrix products, arithmetic and copies ran while one was open for 23% of the time, Pallas kernels for 0%

commit v1 on v0

--- a/solution.py
+++ b/solution.py
@@ -70,7 +70,28 @@
         0.5 * (hidden[0].astype(jnp.float32) + jnp.flip(reverse, 0).astype(jnp.float32))
     ).astype(jnp.bfloat16)
     gathered = lax.all_gather(averaged, "ch", axis=1, tiled=True)
-    weight_rows = lax.all_gather(out_weight, "seq", axis=0, tiled=True)
+    high = lax.psum(1, axis_name="seq")
+    mid_arr, o_now, local_now = (high, lax.axis_index("seq"), out_weight.shape[0])
+    so_far_all = tuple(
+        (src_i * mid_arr if pp == 0 else src_i for pp, src_i in enumerate(out_weight.shape))
+    )
+    piece_next = jnp.zeros(so_far_all, out_weight.dtype)
+    weight_rows = lax.dynamic_update_slice_in_dim(piece_next, out_weight, o_now * local_now, axis=0)
+    n_now = r2 = out_weight
+    for to_i in range(1, mid_arr // 2 + 1):
+        n_now = lax.ppermute(
+            n_now, axis_name="seq", perm=tuple(((pp, (pp + 1) % mid_arr) for pp in range(mid_arr)))
+        )
+        weight_rows = lax.dynamic_update_slice_in_dim(
+            weight_rows, n_now, (o_now - to_i) % mid_arr * local_now, axis=0
+        )
+        if 2 * to_i < mid_arr:
+            r2 = lax.ppermute(
+                r2, axis_name="seq", perm=tuple(((pp, (pp - 1) % mid_arr) for pp in range(mid_arr)))
+            )
+            weight_rows = lax.dynamic_update_slice_in_dim(
+                weight_rows, r2, (o_now + to_i) % mid_arr * local_now, axis=0
+            )
     result = jnp.dot(gathered, weight_rows, preferred_element_type=jnp.float32)
     return result.astype(jnp.bfloat16)
 

time: 465 us -> 413 us (0.89)
  the two profiles are of different devices: /device:TPU:0 before, /device:TPU:6 now
where the time goes in v1:
time: 413 us; the launch traced here: 410 us
  local copies, waits for them, and re-layouts  193 us (47%)
  other arithmetic  91.8 us (22%)
  waiting for transfers between devices  68.6 us (17%)
  starting transfers between devices  23.8 us (6%)
  matrix products  18.9 us (5%)
  between operations  13.9 us (3%)
    gather x2, local copies, waits for them, and re-layouts, toeplitz(): picked = jnp.take(filters, jnp.clip(tap_index, 0, tap_count - 1), axis=0)  75.7 us
    add x1, other arithmetic, per_device(): short_out + short_filter[:, shift_index, :] * extended[:, begin:begin + l...  46.7 us
    ppermute x7, waiting for transfers between devices, per_device(): lax.ppermute(r2, axis_name='seq', perm=tuple(((pp, (pp - 1) % mid_arr) fo...  35.4 us
    ppermute x8, waiting for transfers between devices, per_device(): lax.ppermute(n_now, axis_name='seq', perm=tuple(((pp, (pp + 1) % mid_arr)...  33.2 us
    gather x2, local copies, waits for them, and re-layouts, per_device(): features = jnp.take(corner, strand_bases, axis=0)  30.1 us
    dynamic_update_slice x8, local copies, waits for them, and re-layouts, per_device(): lax.dynamic_update_slice_in_dim(weight_rows, n_now, (o_now - to_i) % mid_...  16 us
    dynamic_update_slice x7, local copies, waits for them, and re-layouts, per_device(): lax.dynamic_update_slice_in_dim(weight_rows, r2, (o_now + to_i) % mid_arr...  13.8 us
    select_n x1, other arithmetic, toeplitz(): jnp.where(inside[:, :, None], picked, jnp.zeros((), filters.dtype))  13.8 us
  transfers between devices with their start and end apart: 20, of which 8 were waited for; matrix products, arithmetic and copies ran while one was open for 70% of the time, Pallas kernels for 0%

profile of v1, /device:TPU:6, one launch (start us, length us, event | category | flops | bytes accessed | tf_op | source)
XLA Modules:
  0.0 409.5 jit_solution(5369000338842051934)
XLA Ops:
  6.5 1.7 collective-permute-start.5
  12.0 17.1 %gather_fusion.1 = bf16[512,3,2048]{2,1,0:T(4,128)(2,1)} fusion(bf16[4,3,2048]{2,1,0:T(4,128)(2,1)S(1)} %copy.31, s32[1024]{0:T(1024)S(1)} %pad_clamp_fusion.1), kind=kCustom, calls=%fused_computation.1 | custom fusion | bytes 12584960 | tf_op jit(solution)/shard_map/jit(_take)/gather | solution.py:43
  29.1 13.0 %copy.32 = bf16[2,256,3,2048]{1,3,0,2:T(8,128)(2,1)} copy(bf16[2,256,3,2048]{3,2,1,0:T(4,128)(2,1)} %bitcast.65) | data formatting | bytes 12582912 | tf_op jit(solution)/shard_map/jit(_take)/gather | solution.py:43
  42.1 3.4 broadcast_select_fusion
  45.5 2.6 copy-done.2
  49.8 1.9 collective-permute-start.1
  52.5 2.6 collective-permute-start
  55.7 65.9 %gather_fusion.2 = bf16[32640,128]{1,0:T(8,128)(2,1)} fusion(bf16[128,128]{1,0:T(8,128)(2,1)S(1)} %copy-done, s32[32768]{0:T(1024)S(1)} %pad_clamp_fusion), kind=kCustom, calls=%fused_computation.2 | custom fusion | bytes 16842240 | tf_op jit(solution)/shard_map/jit(_take)/gather | solution.py:29
  121.6 9.8 %reshape.197 = bf16[128,255,128]{2,1,0:T(8,128)(2,1)} reshape(bf16[32640,128]{1,0:T(8,128)(2,1)} %gather_fusion.2) | data formatting | bytes 16711680 | tf_op jit(solution)/shard_map/jit(_take)/gather | solution.py:29
  134.1 10.4 %maximum_convert_fusion = f32[2,262,3,2048]{1,3,0,2:T(8,128)} fusion(bf16[2,256,3,2048]{1,3,0,2:T(8,128)(2,1)} %copy-done.2, bf16[1,6,3,2048]{1,3,0,2:T(8,128)(2,1)S(1)} %bitcast.68, bf16[1,6,3,2048]{1,3,0,2:T(8,128)(2,1)S(1)} %bitcast.69), kind=kLoop, calls=%fused_computation.16 | loop fusion | flops 19316736 | bytes 19316736 | tf_op jit(solution)/shard_map/convert_element_type | solution.py:45
  144.5 46.7 %fusion = f32[2,256,3,2048]{1,3,0,2:T(8,128)} fusion(f32[2,262,3,2048]{1,3,0,2:T(8,128)} %maximum_convert_fusion, f32[3,2048]{1,0:T(4,128)S(1)} %get-tuple-element.18, f32[3,2048]{1,0:T(4,128)S(1)} %get-tuple-element.19, f32[3,2048]{1,0:T(4,128)S(1)} %get-tuple-element.20, f32[3,2048]{1,0:T(4,128)S(1)} %get-tuple-element.21, ...), kind=kLoop, calls=%fused_computation.4 | loop fusion | flops 40894464 | bytes 100835328 | tf_op jit(solution)/shard_map/add | solution.py:50
  191.2 2.1 collective-permute-start.6
  193.3 3.9 fusion.14
  198.5 2.7 collective-permute-start.3
  201.2 1.9 collective-permute-start.2
  203.2 1.8 collective-permute-start.7
  205.0 18.7 %collective-permute-done.6 = bf16[256,2048]{1,0:T(8,128)(2,1)S(1)} collective-permute-done((bf16[256,2048]{1,0:T(8,128)(2,1)}, bf16[256,2048]{1,0:T(8,128)(2,1)S(1)}, u32[]{:S(2)}, u32[]{:S(2)}) %collective-permute-start.6) | collective-permute-done | bytes 1048608 | tf_op jit(solution)/shard_map/ppermute | solution.py:82
  223.6 13.8 %select_bitcast_fusion = bf16[128,128,255,1,1]{0,2,1,4,3:T(8,128)(2,1)} fusion(bf16[128,255,128]{2,1,0:T(8,128)(2,1)} %reshape.197, pred[128,255]{1,0:T(8,128)(4,1)S(1)} %get-tuple-element.24, pred[128,255]{1,0:T(8,128)(4,1)S(1)} %get-tuple-element.25), kind=kLoop, calls=%fused_computation.17 | loop fusion | flops 8355840 | bytes 16776960 | tf_op jit(solution)/shard_map/jit(_where)/select_n | solution.py:30
  237.8 12.6 %copy.41 = bf16[128,128,255,1,1]{2,1,4,3,0:T(8,128)(2,1)} copy(bf16[128,128,255,1,1]{0,2,1,4,3:T(8,128)(2,1)} %select_bitcast_fusion) | data formatting | bytes 16711680 | tf_op jit(solution)/shard_map/jit(_where)/select_n | solution.py:30
  250.4 6.0 %broadcast_in_dim.49 = bf16[4096,2048]{1,0:T(8,128)(2,1)} broadcast(bf16[]{:T(256)} %constant.136.clone.1), dimensions={} | broadcast | bytes 16777218 | tf_op jit(solution)/shard_map/broadcast_in_dim | solution.py:78
  259.0 4.4 %pad_maximum_fusion.1 = (bf16[2,255,2048]{1,2,0:T(8,128)(2,1)S(1)}, bf16[2,255,2048]{1,2,0:T(8,128)(2,1)}) fusion(bf16[2,256,2048]{1,2,0:T(8,128)(2,1)S(1)} %fusion.14, bf16[1,127,2048]{1,2,0:T(8,128)(2,1)} %bitcast.15, bf16[1,127,2048]{1,2,0:T(8,128)(2,1)} %bitcast.13), kind=kLoop, calls=%fused_computation.30 | loop fusion | flops 6266880 | bytes 9412608 | tf_op jit(solution)/shard_map/concatenate | solution.py:54
  263.4 7.1 %fusion.11 = f32[2,2,128,128,16]{2,4,1,0,3:T(8,128)S(1)} fusion(bf16[128,128,255,1,1]{2,1,4,3,0:T(8,128)(2,1)} %copy.41, bf16[2,1,255,128,16]{2,4,3,0,1:T(8,128)(2,1)} %bitcast.67, bf16[2,1,255,128,16]{2,4,3,0,1:T(8,128)(2,1)S(1)} %bitcast.66), kind=kOutput, calls=%fused_computation.28 | convolution fusion | flops 536862720 | bytes 16728064 | tf_op jit(solution)/shard_map/grw,snwgc->snrgc/dot_general | solution.py:65
  270.4 4.2 %copy.40 = f32[2,2,128,128,16]{2,1,4,3,0:T(2,128)} copy(f32[2,2,128,128,16]{2,4,1,0,3:T(8,128)S(1)} %fusion.11) | data formatting | bytes 8388608 | tf_op jit(solution)/shard_map/grw,snwgc->snrgc/transpose | solution.py:65
  274.6 6.4 %reshape.178 = f32[2,256,2048]{1,2,0:T(8,128)} reshape(f32[2,2,128,128,16]{2,1,4,3,0:T(2,128)} %copy.40) | data formatting | bytes 8388608 | tf_op jit(solution)/shard_map/reshape | solution.py:66
  281.1 1.8 collective-permute-done.9
  282.8 1.9 collective-permute-start.11
  284.7 6.3 %fusion.8 = bf16[2,256,2048]{1,2,0:T(8,128)(2,1)S(1)} fusion(f32[2,256,3,2048]{1,3,0,2:T(8,128)} %fusion, f32[2,256,2048]{1,2,0:T(8,128)} %reshape.178, f32[2048]{0:T(1024)S(1)} %copy-done.7), kind=kLoop, calls=%fused_computation.23 | loop fusion | flops 7340032 | bytes 18882560 | tf_op jit(solution)/shard_map/convert_element_type | solution.py:67
  292.1 13.7 %rev.9 = bf16[256,2048]{0,1:T(8,128)(2,1)S(1)} reverse(bf16[256,2048]{0,1:T(8,128)(2,1)} %slice_bitcast_fusion.3), dimensions={0} | reverse | bytes 2097152 | tf_op jit(solution)/shard_map/jit(_flip)/rev | solution.py:70
  305.8 2.8 collective-permute-done.11
  308.6 1.9 collective-permute-start.13
  311.8 2.3 constant_dynamic-update-slice_fusion.14
  314.1 2.3 constant_dynamic-update-slice_fusion.13
  316.4 2.3 constant_dynamic-update-slice_fusion.12
  318.8 26.8 %collective-permute-done.13 = bf16[256,2048]{1,0:T(8,128)(2,1)} collective-permute-done((bf16[256,2048]{1,0:T(8,128)(2,1)}, bf16[256,2048]{1,0:T(8,128)(2,1)}, u32[]{:S(2)}, u32[]{:S(2)}) %collective-permute-start.13) | collective-permute-done | bytes 1048608 | tf_op jit(solution)/shard_map/ppermute | solution.py:89
  345.6 1.9 collective-permute-start.15
  347.5 2.4 constant_dynamic-update-slice_fusion.11
  349.9 2.3 constant_dynamic-update-slice_fusion.10
  352.2 2.3 constant_dynamic-update-slice_fusion.9
  354.5 2.3 constant_dynamic-update-slice_fusion.8
  356.8 2.3 constant_dynamic-update-slice_fusion.7
  360.1 1.8 collective-permute-start.17
  361.9 2.3 constant_dynamic-update-slice_fusion.6
  364.3 11.3 %collective-permute-done.16 = bf16[256,2048]{1,0:T(8,128)(2,1)S(1)} collective-permute-done((bf16[256,2048]{1,0:T(8,128)(2,1)}, bf16[256,2048]{1,0:T(8,128)(2,1)S(1)}, u32[]{:S(2)}, u32[]{:S(2)}) %collective-permute-start.16) | collective-permute-done | bytes 1048608 | tf_op jit(solution)/shard_map/ppermute | solution.py:82
  375.5 2.4 constant_dynamic-update-slice_fusion.5
  378.0 2.3 constant_dynamic-update-slice_fusion.4
  382.4 3.1 collective-permute-done.17
  386.6 3.2 collective-permute-done.18
  390.8 11.9 %convolution_convert_fusion = bf16[256,2048]{1,0:T(8,128)(2,1)} fusion(bf16[256,4096]{0,1:T(8,128)(2,1)} %all-gather.2.cloned.1.call-done, bf16[4096,2048]{1,0:T(8,128)(2,1)} %constant_dynamic-update-slice_fusion), kind=kOutput, calls=%fused_computation.27 | convolution fusion | flops 4295491584 | bytes 19922944 | tf_op jit(solution)/shard_map/dot_general | solution.py:95
  (68 shorter events, 20.9 us)
Async XLA Ops:
  6.5 49.1 %copy-start = (bf16[128,128]{1,0:T(8,128)(2,1)S(1)}, bf16[128,128]{1,0:T(8,128)(2,1)}, u32[]{:S(2)}) copy-start(bf16[128,128]{1,0:T(8,128)(2,1)} %param.11) | copy-start | bytes 98308
  6.5 384.3 %all-gather.2.cloned.1.call-start = ((), (), s32[]{:S(2)}) async-start(), calls=%async_computation | async-start | bytes 3145728 | tf_op jit(solution)/shard_map/all_gather | solution.py:72
  6.5 184.7 %collective-permute-start.4 = (bf16[256,2048]{1,0:T(8,128)(2,1)}, bf16[256,2048]{1,0:T(8,128)(2,1)}, u32[]{:S(2)}, u32[]{:S(2)}) collective-permute-start(bf16[256,2048]{1,0:T(8,128)(2,1)} %param.13), channel_id=1, source_target_pairs={{0,2},{2,4},{4,6},{6,8},{8,10},{10,12},{12,14},{14,16},{16,18},{18... | collective-permute-start | bytes 3145736 | tf_op jit(solution)/shard_map/ppermute | solution.py:82
  6.5 196.6 %collective-permute-start.5 = (bf16[256,2048]{1,0:T(8,128)(2,1)}, bf16[256,2048]{1,0:T(8,128)(2,1)}, u32[]{:S(2)}, u32[]{:S(2)}) collective-permute-start(bf16[256,2048]{1,0:T(8,128)(2,1)} %param.13), channel_id=1, source_target_pairs={{0,30},{2,0},{4,2},{6,4},{8,6},{10,8},{12,10},{14,12},{16,14},{18,... | collective-permute-start | bytes 3145736 | tf_op jit(solution)/shard_map/ppermute | solution.py:89
  29.1 13.0 %copy-start.6 = (s32[256]{0:T(256)S(1)}, s32[256]{0:T(256)}, u32[]{:S(2)}) copy-start(s32[256]{0:T(256)} %param.8) | copy-start | bytes 3076
  42.1 13.0 %copy-start.5 = (f32[3,7,2048]{2,1,0:T(8,128)S(1)}, f32[3,7,2048]{2,1,0:T(8,128)}, u32[]{:S(2)}) copy-start(f32[3,7,2048]{2,1,0:T(8,128)} %param.10) | copy-start | bytes 516100
  45.5 2.7 copy-start.2
  49.8 81.7 %collective-permute-start.1 = (bf16[6,3,2048]{2,0,1:T(8,128)(2,1)S(1)}, bf16[6,3,2048]{2,0,1:T(8,128)(2,1)S(1)}, u32[]{:S(2)}, u32[]{:S(2)}) collective-permute-start(bf16[6,3,2048]{2,0,1:T(8,128)(2,1)S(1)} %copy.35), channel_id=1, source_target_pairs={{2,0},{4,2},{6,4},{8,6},{10,8},{12,10},{14,12},{16,14},{18,16},{20... | collective-permute-start | bytes 221192 | tf_op jit(solution)/shard_map/ppermute | solution.py:13
  52.5 79.9 %collective-permute-start = (bf16[6,3,2048]{2,0,1:T(8,128)(2,1)S(1)}, bf16[6,3,2048]{2,0,1:T(8,128)(2,1)}, u32[]{:S(2)}, u32[]{:S(2)}) collective-permute-start(bf16[6,3,2048]{2,0,1:T(8,128)(2,1)S(1)} %copy.33), channel_id=1, source_target_pairs={{0,2},{2,4},{4,6},{6,8},{8,10},{10,12},{12,14},{14,16},{16,18},{18... | collective-permute-start | bytes 221192 | tf_op jit(solution)/shard_map/ppermute | solution.py:13
  191.2 32.4 %collective-permute-start.6 = (bf16[256,2048]{1,0:T(8,128)(2,1)}, bf16[256,2048]{1,0:T(8,128)(2,1)S(1)}, u32[]{:S(2)}, u32[]{:S(2)}) collective-permute-start(bf16[256,2048]{1,0:T(8,128)(2,1)} %collective-permute-done.4), channel_id=1, source_target_pairs={{0,2},{2,4},{4,6},{6,8},{8,10},{10,12},{12,14},{14,16},{16,18},{18... | collective-permute-start | bytes 3145736 | tf_op jit(solution)/shard_map/ppermute | solution.py:82
  198.5 60.4 %collective-permute-start.3 = (bf16[127,2048]{0,1:T(8,128)(2,1)}, bf16[127,2048]{0,1:T(8,128)(2,1)}, u32[]{:S(2)}, u32[]{:S(2)}) collective-permute-start(bf16[127,2048]{0,1:T(8,128)(2,1)} %get-tuple-element.10), channel_id=1, source_target_pairs={{2,0},{4,2},{6,4},{8,6},{10,8},{12,10},{14,12},{16,14},{18,16},{20... | collective-permute-start | bytes 1560584 | tf_op jit(solution)/shard_map/ppermute | solution.py:13
  201.2 57.7 %collective-permute-start.2 = (bf16[127,2048]{0,1:T(8,128)(2,1)}, bf16[127,2048]{0,1:T(8,128)(2,1)}, u32[]{:S(2)}, u32[]{:S(2)}) collective-permute-start(bf16[127,2048]{0,1:T(8,128)(2,1)} %get-tuple-element.9), channel_id=1, source_target_pairs={{0,2},{2,4},{4,6},{6,8},{8,10},{10,12},{12,14},{14,16},{16,18},{18... | collective-permute-start | bytes 1560584 | tf_op jit(solution)/shard_map/ppermute | solution.py:13
  203.2 54.3 %collective-permute-start.7 = (bf16[256,2048]{1,0:T(8,128)(2,1)}, bf16[256,2048]{1,0:T(8,128)(2,1)}, u32[]{:S(2)}, u32[]{:S(2)}) collective-permute-start(bf16[256,2048]{1,0:T(8,128)(2,1)} %collective-permute-done.5), channel_id=1, source_target_pairs={{0,30},{2,0},{4,2},{6,4},{8,6},{10,8},{12,10},{14,12},{16,14},{18,... | collective-permute-start | bytes 3145736 | tf_op jit(solution)/shard_map/ppermute | solution.py:89
  223.6 13.9 %copy-start.4 = (bf16[256,2048]{1,0:T(8,128)(2,1)}, bf16[256,2048]{1,0:T(8,128)(2,1)S(1)}, u32[]{:S(2)}) copy-start(bf16[256,2048]{1,0:T(8,128)(2,1)S(1)} %collective-permute-done.6) | copy-start | bytes 3145732
  223.6 35.3 %collective-permute-start.8 = (bf16[256,2048]{1,0:T(8,128)(2,1)S(1)}, bf16[256,2048]{1,0:T(8,128)(2,1)}, u32[]{:S(2)}, u32[]{:S(2)}) collective-permute-start(bf16[256,2048]{1,0:T(8,128)(2,1)S(1)} %collective-permute-done.6), channel_id=1, source_target_pairs={{0,2},{2,4},{4,6},{6,8},{8,10},{10,12},{12,14},{14,16},{16,18},{18... | collective-permute-start | bytes 3145736 | tf_op jit(solution)/shard_map/ppermute | solution.py:82
  250.4 6.0 %copy-start.3 = (bf16[256,2048]{1,0:T(8,128)(2,1)S(1)}, bf16[256,2048]{1,0:T(8,128)(2,1)}, u32[]{:S(2)}) copy-start(bf16[256,2048]{1,0:T(8,128)(2,1)} %param.13) | copy-start | bytes 3145732
  257.5 25.4 %collective-permute-start.9 = (bf16[256,2048]{1,0:T(8,128)(2,1)}, bf16[256,2048]{1,0:T(8,128)(2,1)}, u32[]{:S(2)}, u32[]{:S(2)}) collective-permute-start(bf16[256,2048]{1,0:T(8,128)(2,1)} %collective-permute-done.7), channel_id=1, source_target_pairs={{0,30},{2,0},{4,2},{6,4},{8,6},{10,8},{12,10},{14,12},{16,14},{18,... | collective-permute-start | bytes 3145736 | tf_op jit(solution)/shard_map/ppermute | solution.py:89
  259.0 25.8 %collective-permute-start.10 = (bf16[256,2048]{1,0:T(8,128)(2,1)}, bf16[256,2048]{1,0:T(8,128)(2,1)}, u32[]{:S(2)}, u32[]{:S(2)}) collective-permute-start(bf16[256,2048]{1,0:T(8,128)(2,1)} %collective-permute-done.8), channel_id=1, source_target_pairs={{0,2},{2,4},{4,6},{6,8},{8,10},{10,12},{12,14},{14,16},{16,18},{18... | collective-permute-start | bytes 3145736 | tf_op jit(solution)/shard_map/ppermute | solution.py:82
  270.4 14.3 %copy-start.7 = (f32[2048]{0:T(1024)S(1)}, f32[2048]{0:T(1024)}, u32[]{:S(2)}) copy-start(f32[2048]{0:T(1024)} %param.12) | copy-start | bytes 24580
  282.8 25.8 %collective-permute-start.11 = (bf16[256,2048]{1,0:T(8,128)(2,1)}, bf16[256,2048]{1,0:T(8,128)(2,1)}, u32[]{:S(2)}, u32[]{:S(2)}) collective-permute-start(bf16[256,2048]{1,0:T(8,128)(2,1)} %collective-permute-done.9), channel_id=1, source_target_pairs={{0,30},{2,0},{4,2},{6,4},{8,6},{10,8},{12,10},{14,12},{16,14},{18,... | collective-permute-start | bytes 3145736 | tf_op jit(solution)/shard_map/ppermute | solution.py:89
  284.7 25.8 %collective-permute-start.12 = (bf16[256,2048]{1,0:T(8,128)(2,1)}, bf16[256,2048]{1,0:T(8,128)(2,1)}, u32[]{:S(2)}, u32[]{:S(2)}) collective-permute-start(bf16[256,2048]{1,0:T(8,128)(2,1)} %collective-permute-done.10), channel_id=1, source_target_pairs={{0,2},{2,4},{4,6},{6,8},{8,10},{10,12},{12,14},{14,16},{16,18},{18... | collective-permute-start | bytes 3145736 | tf_op jit(solution)/shard_map/ppermute | solution.py:82
  308.6 37.0 %collective-permute-start.13 = (bf16[256,2048]{1,0:T(8,128)(2,1)}, bf16[256,2048]{1,0:T(8,128)(2,1)}, u32[]{:S(2)}, u32[]{:S(2)}) collective-permute-start(bf16[256,2048]{1,0:T(8,128)(2,1)} %collective-permute-done.11), channel_id=1, source_target_pairs={{0,30},{2,0},{4,2},{6,4},{8,6},{10,8},{12,10},{14,12},{16,14},{18,... | collective-permute-start | bytes 3145736 | tf_op jit(solution)/shard_map/ppermute | solution.py:89
  310.5 39.4 %collective-permute-start.14 = (bf16[256,2048]{1,0:T(8,128)(2,1)}, bf16[256,2048]{1,0:T(8,128)(2,1)}, u32[]{:S(2)}, u32[]{:S(2)}) collective-permute-start(bf16[256,2048]{1,0:T(8,128)(2,1)} %collective-permute-done.12), channel_id=1, source_target_pairs={{0,2},{2,4},{4,6},{6,8},{8,10},{10,12},{12,14},{14,16},{16,18},{18... | collective-permute-start | bytes 3145736 | tf_op jit(solution)/shard_map/ppermute | solution.py:82
  345.6 14.5 %collective-permute-start.15 = (bf16[256,2048]{1,0:T(8,128)(2,1)}, bf16[256,2048]{1,0:T(8,128)(2,1)S(1)}, u32[]{:S(2)}, u32[]{:S(2)}) collective-permute-start(bf16[256,2048]{1,0:T(8,128)(2,1)} %collective-permute-done.13), channel_id=1, source_target_pairs={{0,30},{2,0},{4,2},{6,4},{8,6},{10,8},{12,10},{14,12},{16,14},{18,... | collective-permute-start | bytes 3145736 | tf_op jit(solution)/shard_map/ppermute | solution.py:89
  349.9 25.7 %collective-permute-start.16 = (bf16[256,2048]{1,0:T(8,128)(2,1)}, bf16[256,2048]{1,0:T(8,128)(2,1)S(1)}, u32[]{:S(2)}, u32[]{:S(2)}) collective-permute-start(bf16[256,2048]{1,0:T(8,128)(2,1)} %collective-permute-done.14), channel_id=1, source_target_pairs={{0,2},{2,4},{4,6},{6,8},{8,10},{10,12},{12,14},{14,16},{16,18},{18... | collective-permute-start | bytes 3145736 | tf_op jit(solution)/shard_map/ppermute | solution.py:82
  360.1 25.4 %collective-permute-start.17 = (bf16[256,2048]{1,0:T(8,128)(2,1)S(1)}, bf16[256,2048]{1,0:T(8,128)(2,1)S(1)}, u32[]{:S(2)}, u32[]{:S(2)}) collective-permute-start(bf16[256,2048]{1,0:T(8,128)(2,1)S(1)} %collective-permute-done.15), channel_id=1, source_target_pairs={{0,30},{2,0},{4,2},{6,4},{8,6},{10,8},{12,10},{14,12},{16,14},{18,... | collective-permute-start | bytes 3145736 | tf_op jit(solution)/shard_map/ppermute | solution.py:89
  375.5 14.2 %collective-permute-start.18 = (bf16[256,2048]{1,0:T(8,128)(2,1)S(1)}, bf16[256,2048]{1,0:T(8,128)(2,1)S(1)}, u32[]{:S(2)}, u32[]{:S(2)}) collective-permute-start(bf16[256,2048]{1,0:T(8,128)(2,1)S(1)} %collective-permute-done.16), channel_id=1, source_target_pairs={{0,2},{2,4},{4,6},{6,8},{8,10},{10,12},{12,14},{14,16},{16,18},{18... | collective-permute-start | bytes 3145736 | tf_op jit(solution)/shard_map/ppermute | solution.py:82
  389.8 12.9 %copy-start.1 = (bf16[128,128]{1,0:T(8,128)(2,1)S(1)}, bf16[128,128]{1,0:T(8,128)(2,1)}, u32[]{:S(2)}) copy-start(bf16[128,128]{1,0:T(8,128)(2,1)} %param.11) | copy-start | bytes 98308
Sparse Core Ops, SparseCore 0:
  311.9 31.6 all-gather.1
